TPU v7x, 128 devices: a whole 4x4x4 slice. The times are simulated.
128 devices in a mesh: ctx: 8 (over y_lo, x), resp: 16 (over z, y_hi, core).
Axes of the slice: x: 4, y: 4 (y_hi: 2, y_lo: 2; y = y_hi * 2 + y_lo), z: 4, core: 2. Of those that a mesh axis runs over, the one named last changes fastest.
Arguments:
- query: bfloat16 [16, 1024, 4096], P('resp', 'ctx'), may hold values from -12 to 12
- prompt_keys: bfloat16 [1024, 512], P('ctx'), may hold values from -12 to 12
- prompt_value_rows: bfloat16 [1024, 512], P('ctx'), may hold values from -6 to 6
- response_keys: bfloat16 [16, 1024, 512], P('resp', 'ctx'), may hold values from -6 to 6
- response_values: bfloat16 [16, 1024, 512], P('resp', 'ctx'), may hold values from -6 to 6
- d_out: bfloat16 [16, 1024, 4096], P('resp', 'ctx'), may hold values from -24 to 24
- lengths: int32 [16], P('resp'), may hold values from 256 to 1024, as said below
Outputs:
- d_query: bfloat16 [16, 1024, 4096], P('resp', 'ctx')
- d_resp_keys: bfloat16 [16, 1024, 512], P('resp', 'ctx')
- d_resp_values: bfloat16 [16, 1024, 512], P('resp', 'ctx')
- d_prompt_keys: bfloat16 [1024, 512], P(('ctx', 'resp'))
- d_prompt_values: bfloat16 [1024, 512], P(('ctx', 'resp'))
Inputs may be any that keep to these rules, and one draw needn't show every extreme that they name: `lengths`: every draw has some response of 1024 live tokens.
All inputs are finite; a program needn't handle non-finite values.
Results may differ from a plain program's by a relative error of at most 0.017.
Values may be sent and summed in bfloat16 or wider, within the bound.
A program may use at most 128 MiB of HBM per device.

v0:
```python
import jax
import jax.numpy as jnp
from jax import lax
from jax.sharding import PartitionSpec as P

QUERY_HEADS = 32
KEY_VALUE_HEADS = 4
HEAD_SIZE = 128


def head_scores(query_head_count, key_matrix):
    return jnp.einsum(
        "rhgd,nhd->hgrn", query_head_count, key_matrix, preferred_element_type=jnp.float32
    ) * query_head_count.shape[-1] ** (-0.5)


def stats_merge(carried, scores):
    old_max, old_sum = carried
    new_max = jnp.maximum(old_max, jnp.max(scores, axis=-1))
    new_sum = old_sum * jnp.exp(old_max - new_max) + jnp.sum(
        jnp.exp(scores - new_max[..., None]), axis=-1
    )
    return (new_max, new_sum)


def attend_add(running, scores, log_total, value_matrix):
    probs_low = jnp.exp(scores - log_total[..., None]).astype(jnp.bfloat16)
    return running + jnp.einsum(
        "hgrn,nhd->hgrd", probs_low, value_matrix, preferred_element_type=jnp.float32
    )


def grads_of(query_head_count, g_heads, log_total, delta_row, key_matrix, value_matrix, allowed):
    scale_factor = query_head_count.shape[-1] ** (-0.5)
    scores = head_scores(query_head_count, key_matrix)
    if allowed is not None:
        scores = jnp.where(allowed, scores, -jnp.inf)
    probs = jnp.exp(scores - log_total[..., None])
    probs_low = probs.astype(jnp.bfloat16)
    d_probs = jnp.einsum(
        "rhgd,nhd->hgrn", g_heads, value_matrix, preferred_element_type=jnp.float32
    )
    d_scores = (probs * (d_probs - delta_row[..., None])).astype(jnp.bfloat16)
    d_queries = (
        jnp.einsum("hgrn,nhd->hgrd", d_scores, key_matrix, preferred_element_type=jnp.float32)
        * scale_factor
    )
    d_keys = (
        jnp.einsum("hgrn,rhgd->nhd", d_scores, query_head_count, preferred_element_type=jnp.float32)
        * scale_factor
    )
    d_values = jnp.einsum("hgrn,rhgd->nhd", probs_low, g_heads, preferred_element_type=jnp.float32)
    return (d_queries, d_keys, d_values)


def per_device(
    query, prompt_keys, prompt_value_rows, response_keys, response_values, d_out, lengths
):
    rows_per_context = query.shape[1]
    query_group_size = QUERY_HEADS // KEY_VALUE_HEADS
    feature_width = prompt_keys.shape[1]
    positions = lax.axis_index("ctx") * rows_per_context + jnp.arange(
        rows_per_context, dtype=jnp.int32
    )
    live_rows = positions < lengths[0]
    query_head_count = query[0].reshape(
        rows_per_context, KEY_VALUE_HEADS, query_group_size, HEAD_SIZE
    )
    g_heads = jnp.where(live_rows[:, None], d_out[0], jnp.zeros_like(d_out[0])).reshape(
        rows_per_context, KEY_VALUE_HEADS, query_group_size, HEAD_SIZE
    )
    response_all_keys, response_all_values = (
        lax.all_gather(response_keys, "ctx", axis=1, tiled=True),
        lax.all_gather(response_values, "ctx", axis=1, tiled=True),
    )
    response_length = response_all_keys.shape[1]
    response_key_matrix = response_all_keys[0].reshape(response_length, KEY_VALUE_HEADS, HEAD_SIZE)
    response_value_matrix = response_all_values[0].reshape(
        response_length, KEY_VALUE_HEADS, HEAD_SIZE
    )
    allowed = jnp.arange(response_length, dtype=jnp.int32)[None, :] <= positions[:, None]
    resp_scores = jnp.where(allowed, head_scores(query_head_count, response_key_matrix), -jnp.inf)
    first_max = jnp.max(resp_scores, axis=-1)
    first_sum = jnp.sum(jnp.exp(resp_scores - first_max[..., None]), axis=-1)
    attention_begin = jnp.zeros(
        (KEY_VALUE_HEADS, query_group_size, rows_per_context, HEAD_SIZE), jnp.float32
    )
    complete_keys, complete_values = (
        lax.all_gather(prompt_keys, "ctx", axis=0, tiled=True),
        lax.all_gather(prompt_value_rows, "ctx", axis=0, tiled=True),
    )
    prompt_len = complete_keys.shape[0]
    block_length = min(512, prompt_len)
    count_of_blocks = prompt_len // block_length
    blocked_keys = complete_keys.reshape(count_of_blocks, block_length, KEY_VALUE_HEADS, HEAD_SIZE)
    blocked_values = complete_values.reshape(
        count_of_blocks, block_length, KEY_VALUE_HEADS, HEAD_SIZE
    )

    def stats_step(carried, key_block):
        return (stats_merge(carried, head_scores(query_head_count, key_block)), None)

    (row_max, row_sum), unused_stats = lax.scan(stats_step, (first_max, first_sum), blocked_keys)
    log_total = row_max + jnp.log(row_sum)
    attended = attend_add(attention_begin, resp_scores, log_total, response_value_matrix)

    def values_step(running, blocks):
        return (
            attend_add(running, head_scores(query_head_count, blocks[0]), log_total, blocks[1]),
            None,
        )

    attended, unused_values = lax.scan(values_step, attended, (blocked_keys, blocked_values))
    delta_row = jnp.einsum(
        "rhgd,hgrd->hgr", g_heads.astype(jnp.float32), attended, precision=lax.Precision.HIGHEST
    )
    d_queries, d_resp_k, d_resp_v = grads_of(
        query_head_count,
        g_heads,
        log_total,
        delta_row,
        response_key_matrix,
        response_value_matrix,
        allowed,
    )
    resp_terms = jnp.stack(
        [
            d_resp_k.reshape(response_length, feature_width),
            d_resp_v.reshape(response_length, feature_width),
        ]
    ).astype(jnp.bfloat16)
    resp_summed = lax.psum_scatter(resp_terms, "ctx", scatter_dimension=1, tiled=True).astype(
        jnp.float32
    )

    def grads_step(running, blocks):
        block_dq, block_dk, block_dv = grads_of(
            query_head_count, g_heads, log_total, delta_row, blocks[0], blocks[1], None
        )
        return (running + block_dq, (block_dk, block_dv))

    d_queries, block_grads = lax.scan(grads_step, d_queries, (blocked_keys, blocked_values))
    all_dk = block_grads[0].reshape(prompt_len, feature_width)
    all_dv = block_grads[1].reshape(prompt_len, feature_width)
    prompt_dk, prompt_dv = (
        lax.psum_scatter(all_dk, ("ctx", "resp"), scatter_dimension=0, tiled=True),
        lax.psum_scatter(all_dv, ("ctx", "resp"), scatter_dimension=0, tiled=True),
    )
    d_query = (
        d_queries.transpose(2, 0, 1, 3)
        .reshape(1, rows_per_context, QUERY_HEADS * HEAD_SIZE)
        .astype(jnp.bfloat16)
    )
    d_resp_keys = resp_summed[0].reshape(1, rows_per_context, feature_width).astype(jnp.bfloat16)
    d_resp_values = resp_summed[1].reshape(1, rows_per_context, feature_width).astype(jnp.bfloat16)
    return (
        d_query,
        d_resp_keys,
        d_resp_values,
        prompt_dk.astype(jnp.bfloat16),
        prompt_dv.astype(jnp.bfloat16),
    )


def solution(mesh):
    return jax.shard_map(
        per_device,
        mesh=mesh,
        in_specs=(
            P("resp", "ctx", None),
            P("ctx", None),
            P("ctx", None),
            P("resp", "ctx", None),
            P("resp", "ctx", None),
            P("resp", "ctx", None),
            P("resp"),
        ),
        out_specs=(
            P("resp", "ctx", None),
            P("resp", "ctx", None),
            P("resp", "ctx", None),
            P(("ctx", "resp"), None),
            P(("ctx", "resp"), None),
        ),
        check_vma=False,
    )
```

profile of v0, /device:TPU:0, one launch (start us, length us, event | category | flops | bytes accessed | tf_op | source)
XLA Modules:
  0.0 1572.8 jit_solution(9530342416024374039)
XLA Ops:
  7.2 0.7 all-gather.7.cloned.1.call-update
  7.9 0.7 all-gather.11.cloned.1.call-update
  8.7 1.7 copy.27
  10.4 1.7 copy.34
  12.2 1.6 copy.28
  13.8 0.7 copy.32
  14.5 1.7 copy.38
  17.0 2.3 copy.33
  19.2 2.8 bitcast_convert_fusion.1
  22.0 3.3 copy.72
  25.3 1.3 copy.45
  26.6 24.4 %all-gather.7.cloned.1.call-done = bf16[1024,512]{1,0:T(8,128)(2,1)} async-done(((bf16[128,512]{1,0:T(8,128)(2,1)}), bf16[1024,512]{1,0:T(8,128)(2,1)}) %all-gather.7.cloned.1.call-update) | async-done | bytes 1048592 | tf_op jit(solution)/shard_map/all_gather | solution.py:89
  51.0 1.3 reshape.57
  52.5 38.1 %all-gather.11.cloned.1.call-done = bf16[1024,512]{1,0:T(8,128)(2,1)} async-done(((bf16[128,512]{1,0:T(8,128)(2,1)}), bf16[1024,512]{1,0:T(8,128)(2,1)}) %all-gather.11.cloned.1.call-update) | async-done | bytes 1048592 | tf_op jit(solution)/shard_map/all_gather | solution.py:90
  90.7 2.2 reshape.58
  92.9 2.4 copy.39
  95.2 33.9 %all-gather.5.cloned.1.call-done = bf16[1,1024,512]{1,2,0:T(8,128)(2,1)} async-done(((bf16[1,128,512]{1,2,0:T(8,128)(2,1)}), bf16[1,1024,512]{1,2,0:T(8,128)(2,1)}) %all-gather.5.cloned.1.call-update) | async-done | bytes 1048592 | tf_op jit(solution)/shard_map/all_gather | solution.py:73
  129.2 9.7 fusion.52
  138.8 9.1 exponential_reduce_fusion
  148.0 6.1 while.36
  148.0 1.3 bitcast_reduce_fusion.2
  149.3 1.5 fusion.101
  150.8 1.3 bitcast_reduce_fusion.2
  152.1 1.5 fusion.101
  154.2 16.0 %all-gather.9.cloned.1.call-done = bf16[1,1024,512]{1,2,0:T(8,128)(2,1)} async-done(((bf16[1,128,512]{1,2,0:T(8,128)(2,1)}), bf16[1,1024,512]{1,2,0:T(8,128)(2,1)}) %all-gather.9.cloned.1.call-update) | async-done | bytes 1048592 | tf_op jit(solution)/shard_map/all_gather | solution.py:74
  170.1 11.8 fusion.55
  181.9 11.7 while.37
  182.1 5.7 fusion.106
  188.0 5.7 fusion.106
  193.6 2.8 multiply_reduce_fusion
  196.5 9.7 fusion.50
  206.2 3.2 copy-done.6
  209.4 3.1 convolution_multiply_fusion
  212.5 27.0 %while.38 = (s32[]{:T(128)}, f32[4,8,128,128]{3,2,1,0:T(8,128)S(1)}, f32[2,512,4,128]{3,2,1,0:T(4,128)}, f32[2,512,4,128]{3,2,1,0:T(4,128)}, bf16[2,512,4,128]{3...) while((s32[]{:T(128)}, ...), condition=%wide.region_9.10_spmd, body=%wide.region_8.9_spmd.sunk | while | flops 2702442496 | bytes 100188984 | solution.py:142
  212.5 2.4 fusion.117
  215.0 2.4 fusion.118
  217.4 1.3 fusion.120
  218.7 1.4 fusion.119
  220.1 1.5 copy_dynamic-update-slice_fusion.3
  221.6 1.4 copy-done.10
  223.0 0.6 copy-done.12
  223.5 2.4 multiply_add_fusion.5
  226.0 2.4 fusion.117
  228.5 2.4 fusion.118
  230.9 1.3 fusion.120
  232.2 1.4 fusion.119
  233.6 1.5 copy_dynamic-update-slice_fusion.3
  235.1 1.4 copy-done.10
  237.0 2.4 multiply_add_fusion.5
  239.5 3.1 copy.103
  242.9 11.2 bitcast_convert_fusion
  254.1 2.3 copy.50
  256.4 7.2 fusion.53
  263.6 1.5 copy.49
  265.1 2.8 pad_maximum_fusion
  267.9 3.1 copy.102
  271.2 0.7 copy.46
  271.9 1.3 convert_element_type.48
  273.2 611.2 %reduce-scatter.6.cloned.1.call-done = f32[8,512]{1,0:T(8,128)} async-done(((f32[1024,512]{1,0:T(8,128)}), f32[8,512]{1,0:T(8,128)}) %reduce-scatter.6.cloned.1.call-update) | async-done | bytes 16400 | tf_op jit(solution)/shard_map/reduce_scatter | solution.py:146
  884.4 1.3 convert_element_type.49
  885.7 37.1 %reduce-scatter.4.cloned.1.call-done = bf16[2,128,512]{2,1,0:T(8,128)(2,1)} async-done(((bf16[2,1024,512]{2,1,0:T(8,128)(2,1)}), bf16[2,128,512]{2,1,0:T(8,128)(2,1)}) %reduce-scatter.4.cloned.1.call-update) | async-done | bytes 262160 | tf_op jit(solution)/shard_map/reduce_scatter | solution.py:132
  922.8 1.7 fusion.61
  924.5 639.9 %reduce-scatter.8.cloned.1.call-done = f32[8,512]{1,0:T(8,128)} async-done(((f32[1024,512]{1,0:T(8,128)}), f32[8,512]{1,0:T(8,128)}) %reduce-scatter.8.cloned.1.call-update) | async-done | bytes 16400 | tf_op jit(solution)/shard_map/reduce_scatter | solution.py:147
  1564.5 1.3 convert_element_type.50
  (64 shorter events, 2.1 us)
Async XLA Ops:
  7.2 43.9 %all-gather.7.cloned.1.call-start = ((), (), s32[]{:S(2)}) async-start(), calls=%async_computation.4 | async-start | bytes 1179648 | tf_op jit(solution)/shard_map/all_gather | solution.py:89
  7.9 82.8 %all-gather.11.cloned.1.call-start = ((), (), s32[]{:S(2)}) async-start(), calls=%async_computation.6 | async-start | bytes 1179648 | tf_op jit(solution)/shard_map/all_gather | solution.py:90
  8.6 120.5 %all-gather.5.cloned.1.call-start = ((), (), s32[]{:S(2)}) async-start(), calls=%async_computation.3 | async-start | bytes 1179648 | tf_op jit(solution)/shard_map/all_gather | solution.py:73
  10.4 159.7 %all-gather.9.cloned.1.call-start = ((), (), s32[]{:S(2)}) async-start(), calls=%async_computation.5 | async-start | bytes 1179648 | tf_op jit(solution)/shard_map/all_gather | solution.py:74
  12.1 872.3 %reduce-scatter.6.cloned.1.call-start = ((), (), s32[]{:S(2)}) async-start(), calls=%async_computation.8 | async-start | bytes 2113536 | tf_op jit(solution)/shard_map/reduce_scatter | solution.py:146
  13.8 12.8 copy-start.3
  22.0 29.0 %copy-start.7 = (bf16[128,4,8,128]{0,3,2,1:T(8,128)(2,1)}, bf16[128,4,8,128]{0,3,2,1:T(8,128)(2,1)S(1)}, u32[]{:S(2)}) copy-start(bf16[128,4,8,128]{0,3,2,1:T(8,128)(2,1)S(1)} %get-tuple-element.195) | copy-start | bytes 3145732
  154.1 27.8 %copy-start = (bf16[2,512,4,128]{3,1,2,0:T(8,128)(2,1)}, bf16[2,512,4,128]{3,1,2,0:T(8,128)(2,1)S(1)}, u32[]{:S(2)}) copy-start(bf16[2,512,4,128]{3,1,2,0:T(8,128)(2,1)S(1)} %get-tuple-element.421) | copy-start | bytes 3145732
  196.5 12.9 copy-start.8
  206.2 3.2 copy-start.6
  212.5 2.5 copy-start.2
  212.5 2.5 copy-start.5
  217.4 2.7 copy-start.9
  217.4 2.7 copy-start.11
  218.6 4.9 copy-start.1
  221.6 1.4 copy-start.10
  221.6 2.0 copy-start.12
  226.0 2.5 copy-start.2
  226.0 2.5 copy-start.5
  230.9 2.7 copy-start.9
  230.9 2.7 copy-start.11
  232.2 4.9 copy-start.1
  235.1 1.4 copy-start.10
  235.1 2.0 copy-start.12
  242.6 13.8 copy-start.4
  242.6 680.2 %reduce-scatter.4.cloned.1.call-start = ((), (), s32[]{:S(2)}) async-start(), calls=%async_computation.7 | async-start | bytes 2359296 | tf_op jit(solution)/shard_map/reduce_scatter | solution.py:132
  267.9 1296.6 %reduce-scatter.8.cloned.1.call-start = ((), (), s32[]{:S(2)}) async-start(), calls=%async_computation.9 | async-start | bytes 2113536 | tf_op jit(solution)/shard_map/reduce_scatter | solution.py:147
Sparse Core Ops, SparseCore 0:
  9.6 41.3 all-gather.6
  52.7 37.9 all-gather.10
  92.8 36.3 all-gather.4
  131.2 38.9 all-gather.8
  242.7 641.6 reduce-scatter.5
  886.8 35.9 reduce-scatter.3
  925.3 639.1 reduce-scatter.7
where the time goes:
time: 1580 us; the launch traced here: 1570 us
  waiting for transfers between devices  1400 us (89%)
  matrix products  86.3 us (5%)
  local copies, waits for them, and re-layouts  44.4 us (3%)
  other arithmetic  23.4 us (1%)
    reduce_scatter x1, waiting for transfers between devices, per_device(): lax.psum_scatter(all_dv, ('ctx', 'resp'), scatter_dimension=0, tiled=True)  640 us
    reduce_scatter x1, waiting for transfers between devices, per_device(): lax.psum_scatter(all_dk, ('ctx', 'resp'), scatter_dimension=0, tiled=True)  611 us
    all_gather x1, waiting for transfers between devices, per_device(): lax.all_gather(prompt_value_rows, 'ctx', axis=0, tiled=True)  38.1 us
    reduce_scatter x1, waiting for transfers between devices, per_device(): lax.psum_scatter(resp_terms, 'ctx', scatter_dimension=1, tiled=True)  37.1 us
    all_gather x1, waiting for transfers between devices, per_device(): lax.all_gather(response_keys, 'ctx', axis=1, tiled=True)  33.9 us
  transfers between devices with their start and end apart: 7, of which 7 were waited for; matrix products, arithmetic and copies ran while one was open for 5% of the time, Pallas kernels for 0%

commit v1 on v0

v1 whole, which is shorter than its diff:
```python
import functools

import jax
import jax.numpy as jnp
from jax import lax
from jax.experimental import pallas as pl
from jax.experimental.pallas import tpu as pltpu
from jax.sharding import PartitionSpec as P

F32, BF16 = jnp.float32, jnp.bfloat16
MESH = pl.DeviceIdType.MESH
SCALE = 128 ** -0.5
EXP2_SCALE = SCALE * 1.4426950408889634
BLOCK = 16


def dot(a, b):
    return lax.dot_general(a, b, (((1,), (0,)), ((), ())), preferred_element_type=F32)


def aligned(x, n):
    return x if isinstance(x, int) else pl.multiple_of(x, n)


def wait_bytes(ref, sem):
    pltpu.make_async_copy(ref, ref, sem).wait()


def kernel(
    q_hbm, pk_hbm, pv_hbm, rk_hbm, rv_hbm, g_hbm, len_ref,
    dq_hbm, drk_ref, drv_ref, dpk_ref, dpv_ref,
    q, gm, dq, pstage, kv, term, back, half_in, half_sum, z_in, plane_out, plane_in,
    pt0, pt1, ds0, ds1, s0, s1, dp0, dp1, kt0, kt1, vt0, vt1, qst, gst, bias,
    loc_sem, out_sem, p_send, p_recv, f_send, f_recv, r_send, r_recv, d_send, d_recv,
    h_send, h_recv, z_send, z_recv, x_send, x_recv,
):
    c, r = lax.axis_index("ctx"), lax.axis_index("resp")
    y_lo, x = c // 4, c % 4
    z, y_hi, core = r // 4, (r // 2) % 2, r % 2
    sibling = (c, z * 4 + y_hi * 2 + 1 - core)
    other = 1 - core
    PT, DS, KT, VT, S, DP = [pt0, pt1], [ds0, ds1], [kt0, kt1], [vt0, vt1], [s0, s1], [dp0, dp1]

    loads = []
    for g in range(4):
        cols = pl.ds(g * 128, 128)
        loads.append(pltpu.make_async_copy(rk_hbm.at[:, cols], kv.at[g, 0, 8], loc_sem.at[len(loads)]))
        loads.append(pltpu.make_async_copy(rv_hbm.at[:, cols], kv.at[g, 1, 8], loc_sem.at[len(loads)]))
    loads.append(pltpu.make_async_copy(pk_hbm, pstage.at[0], loc_sem.at[8]))
    loads.append(pltpu.make_async_copy(pv_hbm, pstage.at[1], loc_sem.at[9]))
    q_load = pltpu.make_async_copy(q_hbm, q, loc_sem.at[10])
    g_load = pltpu.make_async_copy(g_hbm, gm, loc_sem.at[11])
    for copy in loads:
        copy.start()
    q_load.start()
    g_load.start()

    barrier = pltpu.get_barrier_semaphore()
    plane_id = c * 2 + y_hi

    def plane_device(step):
        to = (plane_id + step) % 16
        return to // 2, to % 2

    for step in range(1, 16):
        to_c, to_y = plane_device(step)
        pl.semaphore_signal(barrier, inc=1, device_id=(to_c, z * 4 + to_y * 2 + core), device_id_type=MESH)
    for step in range(1, 4):
        to_z = (z + step) % 4
        pl.semaphore_signal(barrier, inc=1, device_id=(c, to_z * 4 + y_hi * 2 + core), device_id_type=MESH)
    pl.semaphore_signal(barrier, inc=1, device_id=sibling, device_id_type=MESH)

    for copy in loads:
        copy.wait()
    for kind in range(2):
        rows = pstage[kind].astype(F32)
        order = [zz * 4 + yy * 2 + cc for cc in range(2) for zz in range(4) for yy in range(2)]
        mixed = jnp.concatenate([rows[8 * o : 8 * o + 8] for o in order], axis=0).astype(BF16)
        pstage[kind] = mixed
    for g in range(4):
        for kind in range(2):
            kv[g, kind, c, pl.ds(pl.multiple_of(core * 64, 64), 64), :] = pstage[
                kind, pl.ds(pl.multiple_of(core * 64, 64), 64), g * 128 : g * 128 + 128
            ]
    pl.semaphore_wait(barrier, 19)

    my_half = pl.ds(pl.multiple_of(core * 64, 64), 64)
    other_half = pl.ds(pl.multiple_of(other * 64, 64), 64)

    def prompt_copy(g, step):
        to_c = (c + step) % 8
        to_y = jnp.where(to_c // 4 == y_lo, y_hi, 1 - y_hi)
        return pltpu.make_async_remote_copy(
            src_ref=kv.at[g, :, c, my_half], dst_ref=kv.at[g, :, c, my_half],
            send_sem=p_send.at[g], recv_sem=p_recv.at[g],
            device_id=(to_c, z * 4 + to_y * 2 + core), device_id_type=MESH,
        )

    def resp_copy(g, step):
        return pltpu.make_async_remote_copy(
            src_ref=kv.at[g, :, 8], dst_ref=kv.at[g, :, 8 + step],
            send_sem=r_send.at[g, step], recv_sem=r_recv.at[g, step],
            device_id=(c + step, r), device_id_type=MESH,
        )

    def send_head(g):
        for step in range(1, 8):
            prompt_copy(g, step).start()
        for step in range(1, 8):
            @pl.when(c + step < 8)
            def _():
                resp_copy(g, step).start()

    def forward_copy(g):
        return pltpu.make_async_remote_copy(
            src_ref=kv.at[g, :, pl.ds(0, 8), my_half], dst_ref=kv.at[g, :, pl.ds(0, 8), my_half],
            send_sem=f_send.at[g], recv_sem=f_recv.at[g], device_id=sibling, device_id_type=MESH,
        )

    def forward_head(g):
        wait_bytes(kv.at[g, :, pl.ds(0, 7), my_half], p_recv.at[g])
        forward_copy(g).start()

    def await_head(g):
        for step in range(1, 8):
            @pl.when(step <= c)
            def _():
                wait_bytes(kv.at[g, :, 8 + step], r_recv.at[g, step])
        wait_bytes(kv.at[g, :, pl.ds(0, 8), other_half], f_recv.at[g])

    send_head(0)

    row = lax.broadcasted_iota(jnp.int32, (128, 1024), 0)
    key = lax.broadcasted_iota(jnp.int32, (128, 1024), 1)
    flag = ((key == row + 1) & (key < 128)) | ((row == 127) & (key >= (c + 1) * 128))
    flag = jnp.where(flag, 1.0, 0.0).astype(BF16)
    kt0[128:, 1024:] = flag
    kt1[128:, 1024:] = flag
    row = lax.broadcasted_iota(jnp.int32, (128, 128), 0)
    key = lax.broadcasted_iota(jnp.int32, (128, 128), 1)
    bias[...] = jnp.where(key >= row, -1e30, 0.0).astype(BF16)
    for step in range(1, 8):
        @pl.when(step > c)
        def _():
            for g in range(4):
                for kind in range(2):
                    kv[g, kind, 8 + step] = jnp.zeros((128, 128), BF16)

        @pl.when(c + step > 7)
        def _():
            for g in range(4):
                back[g, step - 1] = jnp.zeros((2, 128, 128), BF16)

    q_load.wait()
    g_load.wait()
    live = lax.broadcasted_iota(jnp.int32, (128, 128), 0) + c * 128 < len_ref[0]
    for t in range(32):
        cols = pl.ds(t * 128, 128)
        gm[:, cols] = jnp.where(live, gm[:, cols].astype(F32), 0.0).astype(BF16)

    def load_head(g):
        for t in range(16):
            rows = pl.ds(t * 128, 128)
            KT[g % 2][0:128, rows] = kv[g, 0, t].T
            VT[g % 2][:, rows] = kv[g, 1, t].T

    def load_queries(g):
        for t in range(8):
            cols = pl.ds((g * 8 + t) * 128, 128)
            qst[:, pl.ds(t * 128, 128)] = q[:, cols].T
            gst[:, pl.ds(t * 128, 128)] = gm[:, cols].T

    def soft_rows(buf, b, k, j):
        rows = pl.ds(j * BLOCK, BLOCK)
        s = S[buf][rows, :]
        m = jnp.max(s, axis=1, keepdims=True)
        dp = DP[buf][rows, :]
        e = jnp.exp2((s - m) * EXP2_SCALE)
        inv = 1.0 / jnp.sum(e, axis=1, keepdims=True)
        delta = jnp.sum(e * dp, axis=1, keepdims=True) * inv
        p = e * inv
        out = pl.ds(aligned(k * 128 + j * BLOCK, BLOCK), BLOCK)
        PT[b][out, :] = p.astype(BF16)
        DS[b][out, :] = (p * (dp - delta)).astype(BF16)

    def grad_keys(g, k):
        cols = pl.ds(aligned(k * 256, 256), 256)
        dkt = dot(qst[...], DS[g % 2][:, cols]) * SCALE
        term[g, 0, pl.ds(k * 2, 2)] = dkt.astype(BF16).T.reshape(2, 128, 128)

    def grad_values(g, k):
        cols = pl.ds(aligned(k * 256, 256), 256)
        dvt = dot(gst[...], PT[g % 2][:, cols])
        term[g, 1, pl.ds(k * 2, 2)] = dvt.astype(BF16).T.reshape(2, 128, 128)

    def grad_query(g, k):
        rows = pl.ds(aligned(k * 128, 128), 128)
        val = dot(DS[g % 2][rows, :], kv[g, 0].reshape(2048, 128)) * SCALE
        dq[:, pl.ds(aligned((g * 8 + k) * 128, 128), 128)] = val.astype(BF16)

    def unit(soft=None, ahead=None, grads=None):
        steps = 128 // BLOCK
        if ahead is not None:
            g, k, buf = ahead
            cols = pl.ds(aligned((g * 8 + k) * 128, 128), 128)
            qb, gb = q[:, cols], gm[:, cols]
            qx = jnp.concatenate([qb, bias[...]], axis=1)
            kt, vt = KT[g % 2], VT[g % 2]
        for j in range(steps):
            if ahead is not None:
                cols = pl.ds(j * 256, 256)
                if j < 4:
                    S[buf][:, cols] = dot(qb, kt[0:128, cols])
                else:
                    S[buf][:, cols] = dot(qx, kt[:, cols])
                DP[buf][:, cols] = dot(gb, vt[:, cols])
            if soft is not None:
                soft_rows(*soft, j)
            if grads is not None:
                if j == 0:
                    grad_keys(*grads)
                if j == 2:
                    grad_values(*grads)
                if j == 5:
                    grad_query(*grads)

    def back_copy(g, step):
        return pltpu.make_async_remote_copy(
            src_ref=term.at[g, :, 8 + step], dst_ref=back.at[g, step - 1],
            send_sem=d_send.at[g, step], recv_sem=d_recv.at[g, step],
            device_id=(c - step, r), device_id_type=MESH,
        )

    def send_back(g):
        for step in range(1, 8):
            @pl.when(step <= c)
            def _():
                back_copy(g, step).start()

    def finish_back(g):
        for step in range(1, 8):
            @pl.when(c + step < 8)
            def _():
                wait_bytes(back.at[g, step - 1], d_recv.at[g, step])
        cols = pl.ds(g * 128, 128)
        for kind, ref in ((0, drk_ref), (1, drv_ref)):
            total = term[g, kind, 8].astype(F32)
            for step in range(1, 8):
                total = total + back[g, step - 1, kind].astype(F32)
            ref[:, cols] = total.astype(BF16)

    def half_copy(g):
        return pltpu.make_async_remote_copy(
            src_ref=term.at[g, :, pl.ds(0, 8), other_half], dst_ref=half_in.at[g],
            send_sem=h_send.at[g], recv_sem=h_recv.at[g], device_id=sibling, device_id_type=MESH,
        )

    def z_copy(g, step):
        to_z = (z + step) % 4
        return pltpu.make_async_remote_copy(
            src_ref=half_sum.at[g, :, :, to_z], dst_ref=z_in.at[g, step - 1],
            send_sem=z_send.at[g, step], recv_sem=z_recv.at[g, step],
            device_id=(c, to_z * 4 + y_hi * 2 + core), device_id_type=MESH,
        )

    def add_halves(g):
        wait_bytes(half_in.at[g], h_recv.at[g])
        for kind in range(2):
            total = term[g, kind, pl.ds(0, 8), my_half, :].astype(F32) + half_in[g, kind].astype(F32)
            half_sum[g, kind] = total.astype(BF16).reshape(8, 4, 16, 128)
        for step in range(1, 4):
            z_copy(g, step).start()

    def add_z(g):
        for step in range(1, 4):
            wait_bytes(z_in.at[g, step - 1], z_recv.at[g, step])
        total = half_sum[g, :, :, z].astype(F32)
        for step in range(1, 4):
            total = total + z_in[g, step - 1].astype(F32)
        for cc in range(8):
            for yy in range(2):
                rows = slice(yy * 8, yy * 8 + 8)
                tile = jnp.concatenate([total[0, cc, rows], total[1, cc, rows]], axis=0)
                plane_out[cc, yy, g] = tile.astype(BF16)

    def plane_copy(step, heads, turn):
        to_c, to_y = plane_device(step)
        return pltpu.make_async_remote_copy(
            src_ref=plane_out.at[to_c, to_y, heads], dst_ref=plane_in.at[plane_id, heads],
            send_sem=x_send.at[turn], recv_sem=x_recv.at[turn],
            device_id=(to_c, z * 4 + to_y * 2 + core), device_id_type=MESH,
        )

    def plane_send(first, count, turn):
        heads = pl.ds(first, count)
        for step in range(1, 16):
            plane_copy(step, heads, turn).start()
        plane_in[plane_id, heads] = plane_out[c, y_hi, heads]

    def plane_finish(first, count, turn):
        for sem in (x_recv, x_send):
            wait_bytes(plane_in.at[pl.ds(0, 15), pl.ds(first, count)], sem.at[turn])
        for g in range(first, first + count):
            total = jnp.zeros((16, 128), F32)
            for i in range(16):
                total = total + plane_in[i, g].astype(F32)
            cols = pl.ds(g * 128, 128)
            dpk_ref[:, cols] = total[0:8].astype(BF16)
            dpv_ref[:, cols] = total[8:16].astype(BF16)

    def out_copy(g):
        cols = pl.ds(g * 1024, 1024)
        return pltpu.make_async_copy(dq.at[:, cols], dq_hbm.at[:, cols], out_sem.at[g])

    forward_head(0)
    await_head(0)
    load_head(0)
    send_head(1)
    unit(ahead=(0, 0, 0))
    for g in range(4):
        b = g % 2
        if g > 0:
            load_queries(g - 1)

        def grads_of(k):
            return None if g == 0 else (g - 1, k)

        def pair(i, _):
            @pl.when(i == 1)
            def _():
                if g < 3:
                    forward_head(g + 1)
                if g >= 2:
                    add_halves(g - 2)

            k = 2 * i
            unit(soft=(0, b, k), ahead=(g, k + 1, 1), grads=grads_of(k))
            unit(soft=(1, b, k + 1), ahead=(g, k + 2, 0), grads=grads_of(k + 1))
            return 0

        lax.fori_loop(0, 3, pair, 0)
        unit(soft=(0, b, 6), ahead=(g, 7, 1), grads=grads_of(6))
        if g < 3:
            await_head(g + 1)
            load_head(g + 1)
            unit(soft=(1, b, 7), ahead=(g + 1, 0, 0), grads=grads_of(7))
            if g < 2:
                send_head(g + 2)
        else:
            unit(soft=(1, b, 7), grads=grads_of(7))
        if g >= 1:
            send_back(g - 1)
            half_copy(g - 1).start()
            out_copy(g - 1).start()
        if g >= 2:
            add_z(g - 2)

    load_queries(3)

    def prompt_part(k, _):
        grad_keys(3, k)
        grad_values(3, k)
        return 0

    lax.fori_loop(4, 8, prompt_part, 0)
    send_back(3)
    lax.fori_loop(0, 4, prompt_part, 0)
    half_copy(3).start()
    add_halves(2)

    def query_part(k, _):
        grad_query(3, k)
        return 0

    lax.fori_loop(0, 4, query_part, 0)
    add_halves(3)
    lax.fori_loop(4, 8, query_part, 0)
    out_copy(3).start()
    add_z(2)
    plane_send(0, 3, 0)
    for g in range(3):
        finish_back(g)
    add_z(3)
    plane_send(3, 1, 1)
    finish_back(3)
    plane_finish(0, 3, 0)
    plane_finish(3, 1, 1)

    for g in range(4):
        wait_bytes(kv.at[g, :, pl.ds(0, 7), my_half], p_send.at[g])
        wait_bytes(kv.at[g, :, pl.ds(0, 8), my_half], f_send.at[g])
        wait_bytes(half_in.at[g], h_send.at[g])
        for step in range(1, 8):
            @pl.when(c + step < 8)
            def _():
                wait_bytes(kv.at[g, :, 8], r_send.at[g, step])

            @pl.when(step <= c)
            def _():
                wait_bytes(term.at[g, :, 8 + step], d_send.at[g, step])
        for step in range(1, 4):
            wait_bytes(z_in.at[g, step - 1], z_send.at[g, step])
        out_copy(g).wait()


def per_device(query, prompt_keys, prompt_value_rows, response_keys, response_values, d_out, lengths):
    any_spec = pl.BlockSpec(memory_space=pl.ANY)
    vmem = pl.BlockSpec(memory_space=pltpu.VMEM)
    dma = pltpu.SemaphoreType.DMA
    scratch = [
        pltpu.VMEM((128, 4096), BF16),
        pltpu.VMEM((128, 4096), BF16),
        pltpu.VMEM((128, 4096), BF16),
        pltpu.VMEM((2, 128, 512), BF16),
        pltpu.VMEM((4, 2, 16, 128, 128), BF16),
        pltpu.VMEM((4, 2, 16, 128, 128), BF16),
        pltpu.VMEM((4, 7, 2, 128, 128), BF16),
        pltpu.VMEM((4, 2, 8, 64, 128), BF16),
        pltpu.VMEM((4, 2, 8, 4, 16, 128), BF16),
        pltpu.VMEM((4, 3, 2, 8, 16, 128), BF16),
        pltpu.VMEM((8, 2, 4, 16, 128), BF16),
        pltpu.VMEM((16, 4, 16, 128), BF16),
    ]
    scratch += [pltpu.VMEM((1024, 2048), BF16)] * 4
    scratch += [pltpu.VMEM((128, 2048), F32)] * 4
    scratch += [pltpu.VMEM((256, 2048), BF16)] * 2 + [pltpu.VMEM((128, 2048), BF16)] * 2
    scratch += [pltpu.VMEM((128, 1024), BF16)] * 2 + [pltpu.VMEM((128, 128), BF16)]
    scratch += [dma((12,)), dma((4,)), dma((4,)), dma((4,)), dma((4,)), dma((4,))]
    scratch += [dma((4, 8))] * 4 + [dma((4,))] * 2 + [dma((4, 4))] * 2 + [dma((2,))] * 2
    out = pl.pallas_call(
        kernel,
        out_shape=[
            jax.ShapeDtypeStruct((128, 4096), BF16),
            jax.ShapeDtypeStruct((128, 512), BF16),
            jax.ShapeDtypeStruct((128, 512), BF16),
            jax.ShapeDtypeStruct((8, 512), BF16),
            jax.ShapeDtypeStruct((8, 512), BF16),
        ],
        in_specs=[any_spec] * 6 + [pl.BlockSpec(memory_space=pltpu.SMEM)],
        out_specs=[any_spec] + [vmem] * 4,
        scratch_shapes=scratch,
        compiler_params=pltpu.CompilerParams(
            collective_id=0, has_side_effects=True, vmem_limit_bytes=58 * 2**20
        ),
    )(query[0], prompt_keys, prompt_value_rows, response_keys[0], response_values[0], d_out[0], lengths)
    d_query, d_rk, d_rv, d_pk, d_pv = out
    return d_query[None], d_rk[None], d_rv[None], d_pk, d_pv


def solution(mesh):
    return jax.shard_map(
        per_device,
        mesh=mesh,
        in_specs=(
            P("resp", "ctx", None),
            P("ctx", None),
            P("ctx", None),
            P("resp", "ctx", None),
            P("resp", "ctx", None),
            P("resp", "ctx", None),
            P("resp"),
        ),
        out_specs=(
            P("resp", "ctx", None),
            P("resp", "ctx", None),
            P("resp", "ctx", None),
            P(("ctx", "resp"), None),
            P(("ctx", "resp"), None),
        ),
        check_vma=False,
    )
```

time: 1580 us -> 88.1 us (0.06)
  waiting for transfers between devices: 1400 us -> 0 us
  matrix products: 86.3 us -> 0 us
  Pallas kernels: 0 us -> 80.9 us
  local copies, waits for them, and re-layouts: 44.4 us -> 5.27 us
  other arithmetic: 23.4 us -> 0 us
    reduce_scatter x3 -> x0, waiting for transfers between devices: 1290 us -> none  [the longest x1 640 us: per_device(): lax.psum_scatter(all_dv, ('ctx', 'resp'), scatter_dimension=0, tiled=True)]
    all_gather x4 -> x0, waiting for transfers between devices: 112 us -> none  [the longest x1 38.1 us: per_device(): lax.all_gather(prompt_value_rows, 'ctx', axis=0, tiled=True)]
    dot_general x20 -> x0, matrix products: 86.3 us -> none  [the longest x3 23.1 us: attend_add(): jnp.einsum('hgrn,nhd->hgrd', probs_low, value_matrix, preferred_element_t...]
    pallas_call x0 -> x1, Pallas kernels: none -> 80.9 us  [per_device(): pl.pallas_call(kernel, out_shape=[jax.ShapeDtypeStruct((128, 4096), BF16)...]
  transfers between devices with their start and end apart: 7 -> 0, of which waited for: 7 -> 0; matrix products, arithmetic and copies ran while one was open for 5% -> 0% of each run, Pallas kernels for 0% -> 0%
where the time goes in v1:
time: 88.1 us; the launch traced here: 87.5 us
  Pallas kernels  80.9 us (92%)
  local copies, waits for them, and re-layouts  5.27 us (6%)
  between operations  1.3 us (1%)
    pallas_call x1, Pallas kernels, per_device(): pl.pallas_call(kernel, out_shape=[jax.ShapeDtypeStruct((128, 4096), BF16)...  80.9 us
    unnamed x13, local copies, waits for them, and re-layouts  5.27 us

profile of v1, /device:TPU:0, one launch (start us, length us, event | category | flops | bytes accessed | tf_op | source)
XLA Modules:
  0.0 87.5 jit_solution(5526267972548193390)
XLA Ops:
  1.3 80.9 %shard_map.110 = (bf16[128,4096]{1,0:T(8,128)(2,1)}, bf16[128,512]{1,0:T(8,128)(2,1)}, bf16[128,512]{1,0:T(8,128)(2,1)}, bf16[8,512]{1,0:T(8,128)(2,1)}, bf16[8,512]{1,0:T(8,128)(2,1)}) custom-call(bf16[128,4096]{1,0:T(8,128)(2,1)} %bitcast.7, bf16[128,512]{1,0:T(8,128)(2,1)} %pk_hbm.1, bf16[128,512]{1,0:T(8,128)(2,1)} %pv_hbm.1, bf16[128,512]{1,0:T(8,128)(2,1)} %bitcast.10, ...), custom_call_target="tpu_custom_call" | custom-call | tf_op jit(solution)/shard_map/pallas_call | solution.py:430
  82.2 0.0 copy-start.1
  82.2 2.3 %copy.18 = bf16[1,128,4096]{2,1,0:T(8,128)(2,1)} copy(bf16[1,128,4096]{2,1,0:T(8,128)(2,1)} %bitcast.9) | data formatting | bytes 2097152
  84.6 0.0 copy-done.1
  84.6 0.0 copy-start
  84.6 0.7 copy.19
  85.2 0.3 copy-done
  85.5 0.0 copy-start.3
  85.5 0.7 copy.20
  86.2 0.0 copy-done.3
  86.2 0.0 copy-start.2
  86.2 0.6 copy.21
  86.8 0.1 copy-done.2
  86.9 0.6 copy.22
Async XLA Ops:
  82.2 2.3 %copy-start.1 = (bf16[128,512]{1,0:T(8,128)(2,1)S(1)}, bf16[128,512]{1,0:T(8,128)(2,1)}, u32[]{:S(2)}) copy-start(bf16[128,512]{1,0:T(8,128)(2,1)} %get-tuple-element.11) | copy-start | bytes 393220
  84.6 1.0 %copy-start = (bf16[128,512]{1,0:T(8,128)(2,1)S(1)}, bf16[128,512]{1,0:T(8,128)(2,1)}, u32[]{:S(2)}) copy-start(bf16[128,512]{1,0:T(8,128)(2,1)} %get-tuple-element.12) | copy-start | bytes 393220
  85.5 0.7 copy-start.3
  86.2 0.7 copy-start.2

commit v2 on v1

--- a/solution.py
+++ b/solution.py
@@ -12,6 +12,7 @@
 SCALE = 128 ** -0.5
 EXP2_SCALE = SCALE * 1.4426950408889634
 BLOCK = 16
+KEY_ORDER = (4, 6, 0, 2)
 
 
 def dot(a, b):
@@ -29,9 +30,9 @@
 def kernel(
     q_hbm, pk_hbm, pv_hbm, rk_hbm, rv_hbm, g_hbm, len_ref,
     dq_hbm, drk_ref, drv_ref, dpk_ref, dpv_ref,
-    q, gm, dq, pstage, kv, term, back, half_in, half_sum, z_in, plane_out, plane_in,
-    pt0, pt1, ds0, ds1, s0, s1, dp0, dp1, kt0, kt1, vt0, vt1, qst, gst, bias,
-    loc_sem, out_sem, p_send, p_recv, f_send, f_recv, r_send, r_recv, d_send, d_recv,
+    q, gm, dq, pstage, pwide, kv, term, back, half_in, half_sum, z_in, plane_out, plane_in,
+    pt0, pt1, ds0, ds1, s0, s1, dp0, dp1, kt0, kt1, vt0, vt1, qst0, qst1, gst0, gst1, bias,
+    loc_sem, out_sem, p_send, p_recv, a_send, a_recv, f_send, f_recv, r_send, r_recv, d_send, d_recv,
     h_send, h_recv, z_send, z_recv, x_send, x_recv,
 ):
     c, r = lax.axis_index("ctx"), lax.axis_index("resp")
@@ -40,6 +41,7 @@
     sibling = (c, z * 4 + y_hi * 2 + 1 - core)
     other = 1 - core
     PT, DS, KT, VT, S, DP = [pt0, pt1], [ds0, ds1], [kt0, kt1], [vt0, vt1], [s0, s1], [dp0, dp1]
+    QT, GT = [qst0, qst1], [gst0, gst1]
 
     loads = []
     for g in range(4):
@@ -70,30 +72,48 @@
         pl.semaphore_signal(barrier, inc=1, device_id=(c, to_z * 4 + y_hi * 2 + core), device_id_type=MESH)
     pl.semaphore_signal(barrier, inc=1, device_id=sibling, device_id_type=MESH)
 
-    for copy in loads:
-        copy.wait()
-    for kind in range(2):
-        rows = pstage[kind].astype(F32)
-        order = [zz * 4 + yy * 2 + cc for cc in range(2) for zz in range(4) for yy in range(2)]
-        mixed = jnp.concatenate([rows[8 * o : 8 * o + 8] for o in order], axis=0).astype(BF16)
-        pstage[kind] = mixed
-    for g in range(4):
-        for kind in range(2):
-            kv[g, kind, c, pl.ds(pl.multiple_of(core * 64, 64), 64), :] = pstage[
-                kind, pl.ds(pl.multiple_of(core * 64, 64), 64), g * 128 : g * 128 + 128
-            ]
-    pl.semaphore_wait(barrier, 19)
-
     my_half = pl.ds(pl.multiple_of(core * 64, 64), 64)
     other_half = pl.ds(pl.multiple_of(other * 64, 64), 64)
-
-    def prompt_copy(g, step):
+    my_rows = pl.ds(pl.multiple_of(core * 64 + z * 16, 16), 16)
+    loads[8].wait()
+    loads[9].wait()
+    for kind in range(2):
+        pwide[kind] = pstage[kind].astype(F32)
+        parts = [pwide[kind, pl.ds(pl.multiple_of((z * 4 + yy * 2 + core) * 8, 8), 8), :] for yy in range(2)]
+        mine = jnp.concatenate(parts, axis=0).astype(BF16)
+        for g in range(4):
+            kv[g, kind, c, my_rows, :] = mine[:, g * 128 : g * 128 + 128]
+    pl.semaphore_wait(barrier, 19)
+
+    def prompt_copy(turn, step):
+        heads = pl.ds(0, 1) if turn == 0 else pl.ds(1, 3)
         to_c = (c + step) % 8
         to_y = jnp.where(to_c // 4 == y_lo, y_hi, 1 - y_hi)
         return pltpu.make_async_remote_copy(
-            src_ref=kv.at[g, :, c, my_half], dst_ref=kv.at[g, :, c, my_half],
-            send_sem=p_send.at[g], recv_sem=p_recv.at[g],
+            src_ref=kv.at[heads, :, c, my_rows], dst_ref=kv.at[heads, :, c, my_rows],
+            send_sem=p_send.at[turn], recv_sem=p_recv.at[turn],
             device_id=(to_c, z * 4 + to_y * 2 + core), device_id_type=MESH,
+        )
+
+    def prompt_bytes(turn):
+        heads = pl.ds(0, 1) if turn == 0 else pl.ds(1, 3)
+        return kv.at[heads, :, pl.ds(0, 7), pl.ds(0, 16)]
+
+    def column_copy(g, step):
+        to_z = (z + step) % 4
+        return pltpu.make_async_remote_copy(
+            src_ref=kv.at[g, :, pl.ds(0, 8), my_rows], dst_ref=kv.at[g, :, pl.ds(0, 8), my_rows],
+            send_sem=a_send.at[g], recv_sem=a_recv.at[g],
+            device_id=(c, to_z * 4 + y_hi * 2 + core), device_id_type=MESH,
+        )
+
+    def column_bytes(g):
+        return kv.at[g, :, pl.ds(0, 8), pl.ds(0, 48)]
+
+    def forward_copy(g):
+        return pltpu.make_async_remote_copy(
+            src_ref=kv.at[g, :, pl.ds(0, 8), my_half], dst_ref=kv.at[g, :, pl.ds(0, 8), my_half],
+            send_sem=f_send.at[g], recv_sem=f_recv.at[g], device_id=sibling, device_id_type=MESH,
         )
 
     def resp_copy(g, step):
@@ -103,23 +123,23 @@
             device_id=(c + step, r), device_id_type=MESH,
         )
 
-    def send_head(g):
+    def send_prompt(turn):
         for step in range(1, 8):
-            prompt_copy(g, step).start()
+            prompt_copy(turn, step).start()
+
+    def send_column(g):
+        for step in range(1, 4):
+            column_copy(g, step).start()
+
+    def forward_head(g):
+        wait_bytes(column_bytes(g), a_recv.at[g])
+        forward_copy(g).start()
+
+    def send_resp(g):
         for step in range(1, 8):
             @pl.when(c + step < 8)
             def _():
                 resp_copy(g, step).start()
-
-    def forward_copy(g):
-        return pltpu.make_async_remote_copy(
-            src_ref=kv.at[g, :, pl.ds(0, 8), my_half], dst_ref=kv.at[g, :, pl.ds(0, 8), my_half],
-            send_sem=f_send.at[g], recv_sem=f_recv.at[g], device_id=sibling, device_id_type=MESH,
-        )
-
-    def forward_head(g):
-        wait_bytes(kv.at[g, :, pl.ds(0, 7), my_half], p_recv.at[g])
-        forward_copy(g).start()
 
     def await_head(g):
         for step in range(1, 8):
@@ -128,7 +148,10 @@
                 wait_bytes(kv.at[g, :, 8 + step], r_recv.at[g, step])
         wait_bytes(kv.at[g, :, pl.ds(0, 8), other_half], f_recv.at[g])
 
-    send_head(0)
+    send_prompt(0)
+    for copy in loads[:8]:
+        copy.wait()
+    send_resp(0)
 
     row = lax.broadcasted_iota(jnp.int32, (128, 1024), 0)
     key = lax.broadcasted_iota(jnp.int32, (128, 1024), 1)
@@ -158,17 +181,15 @@
         cols = pl.ds(t * 128, 128)
         gm[:, cols] = jnp.where(live, gm[:, cols].astype(F32), 0.0).astype(BF16)
 
-    def load_head(g):
-        for t in range(16):
-            rows = pl.ds(t * 128, 128)
-            KT[g % 2][0:128, rows] = kv[g, 0, t].T
-            VT[g % 2][:, rows] = kv[g, 1, t].T
-
-    def load_queries(g):
-        for t in range(8):
-            cols = pl.ds((g * 8 + t) * 128, 128)
-            qst[:, pl.ds(t * 128, 128)] = q[:, cols].T
-            gst[:, pl.ds(t * 128, 128)] = gm[:, cols].T
+    def load_block(g, t):
+        rows = pl.ds(t * 128, 128)
+        KT[g % 2][0:128, rows] = kv[g, 0, t].T
+        VT[g % 2][:, rows] = kv[g, 1, t].T
+
+    def load_query(g, k):
+        cols = pl.ds((g * 8 + k) * 128, 128)
+        QT[g % 2][:, pl.ds(k * 128, 128)] = q[:, cols].T
+        GT[g % 2][:, pl.ds(k * 128, 128)] = gm[:, cols].T
 
     def soft_rows(buf, b, k, j):
         rows = pl.ds(j * BLOCK, BLOCK)
@@ -183,46 +204,49 @@
         PT[b][out, :] = p.astype(BF16)
         DS[b][out, :] = (p * (dp - delta)).astype(BF16)
 
-    def grad_keys(g, k):
-        cols = pl.ds(aligned(k * 256, 256), 256)
-        dkt = dot(qst[...], DS[g % 2][:, cols]) * SCALE
-        term[g, 0, pl.ds(k * 2, 2)] = dkt.astype(BF16).T.reshape(2, 128, 128)
-
-    def grad_values(g, k):
-        cols = pl.ds(aligned(k * 256, 256), 256)
-        dvt = dot(gst[...], PT[g % 2][:, cols])
-        term[g, 1, pl.ds(k * 2, 2)] = dvt.astype(BF16).T.reshape(2, 128, 128)
+    def grad_keys(g, k, kind):
+        cols = pl.ds(k * 256, 512)
+        if kind == 0:
+            val = dot(QT[g % 2][...], DS[g % 2][:, cols]) * SCALE
+        else:
+            val = dot(GT[g % 2][...], PT[g % 2][:, cols])
+        term[g, kind, pl.ds(k * 2, 4)] = val.astype(BF16).T.reshape(4, 128, 128)
 
     def grad_query(g, k):
         rows = pl.ds(aligned(k * 128, 128), 128)
         val = dot(DS[g % 2][rows, :], kv[g, 0].reshape(2048, 128)) * SCALE
         dq[:, pl.ds(aligned((g * 8 + k) * 128, 128), 128)] = val.astype(BF16)
 
-    def unit(soft=None, ahead=None, grads=None):
+    def unit(soft=None, ahead=None, grads=None, load=None):
         steps = 128 // BLOCK
         if ahead is not None:
-            g, k, buf = ahead
-            cols = pl.ds(aligned((g * 8 + k) * 128, 128), 128)
+            g, k = ahead
+            cols = pl.ds((g * 8 + k) * 128, 128)
             qb, gb = q[:, cols], gm[:, cols]
             qx = jnp.concatenate([qb, bias[...]], axis=1)
             kt, vt = KT[g % 2], VT[g % 2]
+            s_ref, dp_ref = S[k % 2], DP[k % 2]
         for j in range(steps):
+            if load is not None:
+                for t in range(2 * j, 2 * j + 2):
+                    load_block(load, t)
             if ahead is not None:
                 cols = pl.ds(j * 256, 256)
                 if j < 4:
-                    S[buf][:, cols] = dot(qb, kt[0:128, cols])
+                    s_ref[:, cols] = dot(qb, kt[0:128, cols])
                 else:
-                    S[buf][:, cols] = dot(qx, kt[:, cols])
-                DP[buf][:, cols] = dot(gb, vt[:, cols])
+                    s_ref[:, cols] = dot(qx, kt[:, cols])
+                dp_ref[:, cols] = dot(gb, vt[:, cols])
             if soft is not None:
-                soft_rows(*soft, j)
+                soft_rows(soft[1] % 2, soft[0] % 2, soft[1], j)
             if grads is not None:
-                if j == 0:
-                    grad_keys(*grads)
-                if j == 2:
-                    grad_values(*grads)
-                if j == 5:
-                    grad_query(*grads)
+                g1, k1 = grads
+                if k1 < 4 and j in (0, 4):
+                    grad_keys(g1, KEY_ORDER[k1], j // 4)
+                if k1 >= 4 and j in (0, 4):
+                    grad_query(g1, 2 * (k1 - 4) + j // 4)
+            if soft is not None and j == 6:
+                load_query(*soft)
 
     def back_copy(g, step):
         return pltpu.make_async_remote_copy(
@@ -312,82 +336,74 @@
         cols = pl.ds(g * 1024, 1024)
         return pltpu.make_async_copy(dq.at[:, cols], dq_hbm.at[:, cols], out_sem.at[g])
 
+    wait_bytes(prompt_bytes(0), p_recv.at[0])
+    send_column(0)
+    send_prompt(1)
     forward_head(0)
+    send_resp(1)
+    wait_bytes(prompt_bytes(1), p_recv.at[1])
+    send_column(1)
     await_head(0)
-    load_head(0)
-    send_head(1)
-    unit(ahead=(0, 0, 0))
+    send_resp(2)
+    send_column(2)
+    for t in range(16):
+        load_block(0, t)
+    unit(ahead=(0, 0))
     for g in range(4):
-        b = g % 2
-        if g > 0:
-            load_queries(g - 1)
-
-        def grads_of(k):
-            return None if g == 0 else (g - 1, k)
-
-        def pair(i, _):
-            @pl.when(i == 1)
-            def _():
+        for k in range(8):
+            if k == 2:
                 if g < 3:
                     forward_head(g + 1)
+                if g >= 1:
+                    send_back(g - 1)
                 if g >= 2:
-                    add_halves(g - 2)
-
-            k = 2 * i
-            unit(soft=(0, b, k), ahead=(g, k + 1, 1), grads=grads_of(k))
-            unit(soft=(1, b, k + 1), ahead=(g, k + 2, 0), grads=grads_of(k + 1))
-            return 0
-
-        lax.fori_loop(0, 3, pair, 0)
-        unit(soft=(0, b, 6), ahead=(g, 7, 1), grads=grads_of(6))
-        if g < 3:
-            await_head(g + 1)
-            load_head(g + 1)
-            unit(soft=(1, b, 7), ahead=(g + 1, 0, 0), grads=grads_of(7))
-            if g < 2:
-                send_head(g + 2)
-        else:
-            unit(soft=(1, b, 7), grads=grads_of(7))
+                    add_z(g - 2)
+            if k == 4 and g >= 1:
+                half_copy(g - 1).start()
+            if k == 6:
+                if g < 3:
+                    await_head(g + 1)
+                if g == 0:
+                    send_resp(3)
+                    send_column(3)
+                if g >= 1:
+                    add_halves(g - 1)
+            ahead = (g, k + 1) if k < 7 else (g + 1, 0) if g < 3 else None
+            unit(
+                soft=(g, k), ahead=ahead, grads=(g - 1, k) if g > 0 else None,
+                load=g + 1 if k == 6 and g < 3 else None,
+            )
         if g >= 1:
-            send_back(g - 1)
-            half_copy(g - 1).start()
             out_copy(g - 1).start()
-        if g >= 2:
-            add_z(g - 2)
-
-    load_queries(3)
-
-    def prompt_part(k, _):
-        grad_keys(3, k)
-        grad_values(3, k)
-        return 0
-
-    lax.fori_loop(4, 8, prompt_part, 0)
+
+    for k in KEY_ORDER[2:]:
+        grad_keys(3, k, 0)
+        grad_keys(3, k, 1)
+    half_copy(3).start()
+    for k in KEY_ORDER[:2]:
+        grad_keys(3, k, 0)
+        grad_keys(3, k, 1)
     send_back(3)
-    lax.fori_loop(0, 4, prompt_part, 0)
-    half_copy(3).start()
-    add_halves(2)
-
-    def query_part(k, _):
-        grad_query(3, k)
-        return 0
-
-    lax.fori_loop(0, 4, query_part, 0)
     add_halves(3)
-    lax.fori_loop(4, 8, query_part, 0)
-    out_copy(3).start()
     add_z(2)
     plane_send(0, 3, 0)
+    for k in range(4):
+        grad_query(3, k)
+    for k in range(4, 8):
+        grad_query(3, k)
+    out_copy(3).start()
+    add_z(3)
+    plane_send(3, 1, 1)
     for g in range(3):
         finish_back(g)
-    add_z(3)
-    plane_send(3, 1, 1)
+    plane_finish(0, 3, 0)
     finish_back(3)
-    plane_finish(0, 3, 0)
     plane_finish(3, 1, 1)
 
+    for turn in range(2):
+        wait_bytes(prompt_bytes(turn), p_send.at[turn])
     for g in range(4):
-        wait_bytes(kv.at[g, :, pl.ds(0, 7), my_half], p_send.at[g])
+        wait_bytes(column_bytes(g), a_send.at[g])
         wait_bytes(kv.at[g, :, pl.ds(0, 8), my_half], f_send.at[g])
         wait_bytes(half_in.at[g], h_send.at[g])
         for step in range(1, 8):
@@ -401,6 +417,27 @@
         for step in range(1, 4):
             wait_bytes(z_in.at[g, step - 1], z_send.at[g, step])
         out_copy(g).wait()
+
+
+def hand_over(*refs):
+    ins, outs, bufs, in_sem, out_sem = refs[:5], refs[5:10], refs[10:15], refs[15], refs[16]
+    quarters = [(0, pl.ds(i * 1024, 1024)) for i in range(4)]
+    parts = quarters + [(i, pl.ds(0, 512)) for i in range(1, 5)]
+    reads = [
+        pltpu.make_async_copy(ins[i].at[:, cols], bufs[i].at[:, cols], in_sem.at[n])
+        for n, (i, cols) in enumerate(parts)
+    ]
+    writes = [
+        pltpu.make_async_copy(bufs[i].at[:, cols], outs[i].at[:, cols], out_sem.at[n])
+        for n, (i, cols) in enumerate(parts)
+    ]
+    for copy in reads:
+        copy.start()
+    for read, write in zip(reads, writes):
+        read.wait()
+        write.start()
+    for copy in writes:
+        copy.wait()
 
 
 def per_device(query, prompt_keys, prompt_value_rows, response_keys, response_values, d_out, lengths):
@@ -412,6 +449,7 @@
         pltpu.VMEM((128, 4096), BF16),
         pltpu.VMEM((128, 4096), BF16),
         pltpu.VMEM((2, 128, 512), BF16),
+        pltpu.VMEM((2, 128, 512), F32),
         pltpu.VMEM((4, 2, 16, 128, 128), BF16),
         pltpu.VMEM((4, 2, 16, 128, 128), BF16),
         pltpu.VMEM((4, 7, 2, 128, 128), BF16),
@@ -424,8 +462,8 @@
     scratch += [pltpu.VMEM((1024, 2048), BF16)] * 4
     scratch += [pltpu.VMEM((128, 2048), F32)] * 4
     scratch += [pltpu.VMEM((256, 2048), BF16)] * 2 + [pltpu.VMEM((128, 2048), BF16)] * 2
-    scratch += [pltpu.VMEM((128, 1024), BF16)] * 2 + [pltpu.VMEM((128, 128), BF16)]
-    scratch += [dma((12,)), dma((4,)), dma((4,)), dma((4,)), dma((4,)), dma((4,))]
+    scratch += [pltpu.VMEM((128, 1024), BF16)] * 4 + [pltpu.VMEM((128, 128), BF16)]
+    scratch += [dma((12,)), dma((4,)), dma((2,)), dma((2,)), dma((4,)), dma((4,)), dma((4,)), dma((4,))]
     scratch += [dma((4, 8))] * 4 + [dma((4,))] * 2 + [dma((4, 4))] * 2 + [dma((2,))] * 2
     out = pl.pallas_call(
         kernel,
@@ -440,10 +478,16 @@
         out_specs=[any_spec] + [vmem] * 4,
         scratch_shapes=scratch,
         compiler_params=pltpu.CompilerParams(
-            collective_id=0, has_side_effects=True, vmem_limit_bytes=58 * 2**20
+            collective_id=0, has_side_effects=True, vmem_limit_bytes=62 * 2**20
         ),
     )(query[0], prompt_keys, prompt_value_rows, response_keys[0], response_values[0], d_out[0], lengths)
-    d_query, d_rk, d_rv, d_pk, d_pv = out
+    d_query, d_rk, d_rv, d_pk, d_pv = pl.pallas_call(
+        hand_over,
+        out_shape=[jax.ShapeDtypeStruct(a.shape, a.dtype) for a in out],
+        in_specs=[any_spec] * 5,
+        out_specs=[any_spec] * 5,
+        scratch_shapes=[pltpu.VMEM(a.shape, a.dtype) for a in out] + [dma((8,)), dma((8,))],
+    )(*out)
     return d_query[None], d_rk[None], d_rv[None], d_pk, d_pv
 
 

time: 88.1 us -> 77.4 us (0.88)
  Pallas kernels: 80.9 us -> 75.5 us
  local copies, waits for them, and re-layouts: 5.27 us -> 0 us
    pallas_call x1, Pallas kernels: 80.9 us -> 73.4 us  [per_device(): pl.pallas_call(kernel, out_shape=[jax.ShapeDtypeStruct((128, 4096), BF16)...]
    unnamed x13 -> x0, local copies, waits for them, and re-layouts: 5.27 us -> none
    pallas_call x0 -> x1, Pallas kernels: none -> 2.14 us  [per_device(): pl.pallas_call(hand_over, out_shape=[jax.ShapeDtypeStruct(a.shape, a.dtyp...]
where the time goes in v2:
time: 77.4 us; the launch traced here: 77 us
  Pallas kernels  75.5 us (98%)
  between operations  1.47 us (2%)
    pallas_call x1, Pallas kernels, per_device(): pl.pallas_call(kernel, out_shape=[jax.ShapeDtypeStruct((128, 4096), BF16)...  73.4 us
    pallas_call x1, Pallas kernels, per_device(): pl.pallas_call(hand_over, out_shape=[jax.ShapeDtypeStruct(a.shape, a.dtyp...  2.14 us

profile of v2, /device:TPU:0, one launch (start us, length us, event | category | flops | bytes accessed | tf_op | source)
XLA Modules:
  0.0 77.0 jit_solution(3120583888674880071)
XLA Ops:
  1.3 73.4 %shard_map.110 = (bf16[128,4096]{1,0:T(8,128)(2,1)}, bf16[128,512]{1,0:T(8,128)(2,1)}, bf16[128,512]{1,0:T(8,128)(2,1)}, bf16[8,512]{1,0:T(8,128)(2,1)}, bf16[8,512]{1,0:T(8,128)(2,1)}) custom-call(bf16[128,4096]{1,0:T(8,128)(2,1)} %bitcast.7, bf16[128,512]{1,0:T(8,128)(2,1)} %pk_hbm.1, bf16[128,512]{1,0:T(8,128)(2,1)} %pv_hbm.1, bf16[128,512]{1,0:T(8,128)(2,1)} %bitcast.9, ...), custom_call_target="tpu_custom_call" | custom-call | tf_op jit(solution)/shard_map/pallas_call | solution.py:468
  74.7 2.1 %shard_map.111 = (bf16[128,4096]{1,0:T(8,128)(2,1)}, bf16[128,512]{1,0:T(8,128)(2,1)}, bf16[128,512]{1,0:T(8,128)(2,1)}, bf16[8,512]{1,0:T(8,128)(2,1)}, bf16[8,512]{1,0:T(8,128)(2,1)}) custom-call(bf16[128,4096]{1,0:T(8,128)(2,1)} %get-tuple-element.15.refs_0_, bf16[128,512]{1,0:T(8,128)(2,1)} %get-tuple-element.16.refs_1_, ...), custom_call_target="tpu_custom_call" | custom-call | tf_op jit(solution)/shard_map/pallas_call | solution.py:484

commit v3 on v2

v3 whole, which is shorter than its diff:
```python
import functools

import jax
import jax.numpy as jnp
from jax import lax
from jax.experimental import pallas as pl
from jax.experimental.pallas import tpu as pltpu
from jax.sharding import PartitionSpec as P

F32, BF16 = jnp.float32, jnp.bfloat16
MESH = pl.DeviceIdType.MESH
SCALE = 128 ** -0.5
EXP2_SCALE = SCALE * 1.4426950408889634
BLOCK = 16
RELAY_AT = {(0, 2): 2, (1, 1): 3}
ROWS = 256


def dot(a, b):
    return lax.dot_general(a, b, (((1,), (0,)), ((), ())), preferred_element_type=F32)


def aligned(x, n):
    return x if isinstance(x, int) else pl.multiple_of(x, n)


def wait_bytes(ref, sem):
    pltpu.make_async_copy(ref, ref, sem).wait()


def kernel(
    q_hbm, pk_hbm, pv_hbm, rk_hbm, rv_hbm, g_hbm, len_ref,
    dq_hbm, drk_ref, drv_ref, dpk_ref, dpv_ref,
    q, gm, dq, pstage, pwide, kv, term, back, half_in, half_sum, z_in, plane_out, plane_in,
    pt0, pt1, ds0, ds1, s0, s1, dp0, dp1, kt0, kt1, vt0, vt1, qst0, qst1, gst0, gst1, bias,
    loc_sem, out_sem, p_send, p_recv, a_send, a_recv, f_send, f_recv, r_send, r_recv, d_send, d_recv,
    h_send, h_recv, z_send, z_recv, x_send, x_recv, y_send,
):
    c, r = lax.axis_index("ctx"), lax.axis_index("resp")
    y_lo, x = c // 4, c % 4
    z, y_hi, core = r // 4, (r // 2) % 2, r % 2
    sibling = (c, z * 4 + y_hi * 2 + 1 - core)
    other = 1 - core
    PT, DS, KT, VT, S, DP = [pt0, pt1], [ds0, ds1], [kt0, kt1], [vt0, vt1], [s0, s1], [dp0, dp1]
    QT, GT = [qst0, qst1], [gst0, gst1]

    loads = []
    for g in range(4):
        cols = pl.ds(g * 128, 128)
        loads.append(pltpu.make_async_copy(rk_hbm.at[:, cols], kv.at[g, 0, 8], loc_sem.at[len(loads)]))
        loads.append(pltpu.make_async_copy(rv_hbm.at[:, cols], kv.at[g, 1, 8], loc_sem.at[len(loads)]))
    loads.append(pltpu.make_async_copy(pk_hbm, pstage.at[0], loc_sem.at[8]))
    loads.append(pltpu.make_async_copy(pv_hbm, pstage.at[1], loc_sem.at[9]))
    q_load = pltpu.make_async_copy(q_hbm, q, loc_sem.at[10])
    g_load = pltpu.make_async_copy(g_hbm, gm, loc_sem.at[11])
    for copy in loads[8:] + loads[:8]:
        copy.start()
    q_load.start()
    g_load.start()

    barrier = pltpu.get_barrier_semaphore()
    plane_id = c * 2 + y_hi

    def plane_device(step):
        to = (plane_id + step) % 16
        return to // 2, to % 2

    for step in range(1, 16):
        to_c, to_y = plane_device(step)
        pl.semaphore_signal(barrier, inc=1, device_id=(to_c, z * 4 + to_y * 2 + core), device_id_type=MESH)
    for step in range(1, 4):
        to_z = (z + step) % 4
        pl.semaphore_signal(barrier, inc=1, device_id=(c, to_z * 4 + y_hi * 2 + core), device_id_type=MESH)
    pl.semaphore_signal(barrier, inc=1, device_id=sibling, device_id_type=MESH)

    my_half = pl.ds(pl.multiple_of(core * 64, 64), 64)
    other_half = pl.ds(pl.multiple_of(other * 64, 64), 64)
    my_rows = pl.ds(pl.multiple_of(core * 64 + z * 16, 16), 16)
    far_z = (z + 2) % 4
    far_rows = pl.ds(pl.multiple_of(core * 64 + far_z * 16, 16), 16)
    loads[8].wait()
    loads[9].wait()
    for kind in range(2):
        pwide[kind] = pstage[kind].astype(F32)
        for zz, rows in ((z, my_rows), (far_z, far_rows)):
            parts = [pwide[kind, pl.ds(pl.multiple_of((zz * 4 + yy * 2 + core) * 8, 8), 8), :] for yy in range(2)]
            mine = jnp.concatenate(parts, axis=0).astype(BF16)
            for g in range(4):
                kv[g, kind, c, rows, :] = mine[:, g * 128 : g * 128 + 128]
    pl.semaphore_wait(barrier, 19)

    def prompt_copy(turn, step, rows):
        heads = pl.ds(0, 1) if turn == 0 else pl.ds(1, 3)
        to_c = (c + step) % 8
        to_y = jnp.where(to_c // 4 == y_lo, y_hi, 1 - y_hi)
        return pltpu.make_async_remote_copy(
            src_ref=kv.at[heads, :, c, rows], dst_ref=kv.at[heads, :, c, rows],
            send_sem=p_send.at[turn], recv_sem=p_recv.at[turn],
            device_id=(to_c, z * 4 + to_y * 2 + core), device_id_type=MESH,
        )

    def prompt_bytes(turn):
        heads = pl.ds(0, 1) if turn == 0 else pl.ds(1, 3)
        return kv.at[heads, :, pl.ds(0, 7), pl.ds(0, 32)]

    def column_copy(g, step):
        to_z = (z + step) % 4
        return pltpu.make_async_remote_copy(
            src_ref=kv.at[g, :, pl.ds(0, 8), my_rows], dst_ref=kv.at[g, :, pl.ds(0, 8), my_rows],
            send_sem=a_send.at[g], recv_sem=a_recv.at[g],
            device_id=(c, to_z * 4 + y_hi * 2 + core), device_id_type=MESH,
        )

    def column_bytes(g):
        return kv.at[g, :, pl.ds(0, 8), pl.ds(0, 32)]

    def forward_copy(g):
        return pltpu.make_async_remote_copy(
            src_ref=kv.at[g, :, pl.ds(0, 8), my_half], dst_ref=kv.at[g, :, pl.ds(0, 8), my_half],
            send_sem=f_send.at[g], recv_sem=f_recv.at[g], device_id=sibling, device_id_type=MESH,
        )

    def resp_copy(g, step):
        return pltpu.make_async_remote_copy(
            src_ref=kv.at[g, :, 8], dst_ref=kv.at[g, :, 8 + step],
            send_sem=r_send.at[g, step], recv_sem=r_recv.at[g, step],
            device_id=(c + step, r), device_id_type=MESH,
        )

    def send_prompt(turn):
        for step in range(1, 8):
            prompt_copy(turn, step, my_rows).start()
            prompt_copy(turn, step, far_rows).start()

    def send_column(g):
        for step in (1, 3):
            column_copy(g, step).start()

    def forward_head(g):
        wait_bytes(column_bytes(g), a_recv.at[g])
        forward_copy(g).start()

    def send_resp(g):
        for step in range(1, 4):
            @pl.when(x + step < 4)
            def _():
                resp_copy(g, step).start()

        @pl.when(y_lo == 0)
        def _():
            resp_copy(g, 4).start()

    def down_copy(g, step):
        return pltpu.make_async_remote_copy(
            src_ref=kv.at[g, :, 8 + step], dst_ref=kv.at[g, :, 12 + step],
            send_sem=y_send.at[g, step], recv_sem=r_recv.at[g, 4 + step],
            device_id=(c + 4, r), device_id_type=MESH,
        )

    def side_copy(g, step):
        return pltpu.make_async_remote_copy(
            src_ref=kv.at[g, :, 12], dst_ref=kv.at[g, :, 12 - step],
            send_sem=y_send.at[g, step], recv_sem=r_recv.at[g, 4 - step],
            device_id=(c - step, r), device_id_type=MESH,
        )

    def wrap_copy(g):
        return pltpu.make_async_remote_copy(
            src_ref=kv.at[g, :, 12], dst_ref=kv.at[g, :, 15],
            send_sem=y_send.at[g, 4], recv_sem=r_recv.at[g, 7],
            device_id=(c + 3, r), device_id_type=MESH,
        )

    def relays(g, act):
        for step in range(1, 4):
            @pl.when((y_lo == 0) & (step <= x))
            def _():
                if act:
                    wait_bytes(kv.at[g, :, 8 + step], r_recv.at[g, step])

            if step < 3:
                @pl.when((y_lo == 0) & (step <= x))
                def _():
                    if act:
                        down_copy(g, step).start()
                    else:
                        wait_bytes(kv.at[g, :, 8], y_send.at[g, step])

        @pl.when(y_lo == 1)
        def _():
            if act:
                wait_bytes(kv.at[g, :, 12], r_recv.at[g, 4])

        for step in range(1, 4):
            @pl.when((y_lo == 1) & (step <= x))
            def _():
                if act:
                    side_copy(g, step).start()
                else:
                    wait_bytes(kv.at[g, :, 8], y_send.at[g, step])

        @pl.when((y_lo == 1) & (x == 0))
        def _():
            if act:
                wrap_copy(g).start()
            else:
                wait_bytes(kv.at[g, :, 8], y_send.at[g, 4])

    def await_head(g):
        for step in (1, 2, 3, 5, 6, 7):
            @pl.when((y_lo == 1) & (step <= c))
            def _():
                wait_bytes(kv.at[g, :, 8 + step], r_recv.at[g, step])
        wait_bytes(kv.at[g, :, pl.ds(0, 8), other_half], f_recv.at[g])

    send_prompt(0)
    for copy in loads[:8]:
        copy.wait()
    send_resp(0)

    def load_block(g, t):
        rows = pl.ds(t * 128, 128)
        KT[g % 2][0:128, rows] = kv[g, 0, t].T
        VT[g % 2][:, rows] = kv[g, 1, t].T

    def load_query(g, k):
        for h in range(2 * k, 2 * k + 2):
            cols = pl.ds((g * 8 + h) * 128, 128)
            QT[g % 2][:, pl.ds(h * 128, 128)] = q[:, cols].T
            GT[g % 2][:, pl.ds(h * 128, 128)] = gm[:, cols].T

    def soft_rows(buf, b, k, j):
        rows = pl.ds(j * BLOCK, BLOCK)
        s = S[buf][rows, :]
        m = jnp.max(s, axis=1, keepdims=True)
        dp = DP[buf][rows, :]
        e = jnp.exp2((s - m) * EXP2_SCALE)
        inv = 1.0 / jnp.sum(e, axis=1, keepdims=True)
        delta = jnp.sum(e * dp, axis=1, keepdims=True) * inv
        p = e * inv
        out = pl.ds(k * ROWS + j * BLOCK, BLOCK)
        PT[b][out, :] = p.astype(BF16)
        DS[b][out, :] = (p * (dp - delta)).astype(BF16)

    def grad_keys(g, k, kind):
        cols = pl.ds(k * 256, 512)
        if kind == 0:
            val = dot(QT[g % 2][...], DS[g % 2][:, cols]) * SCALE
        else:
            val = dot(GT[g % 2][...], PT[g % 2][:, cols])
        term[g, kind, pl.ds(k * 2, 4)] = val.astype(BF16).T.reshape(4, 128, 128)

    def grad_query(g, k):
        rows = pl.ds(k * ROWS, ROWS)
        val = dot(DS[g % 2][rows, :], kv[g, 0].reshape(2048, 128)) * SCALE
        for h in range(2):
            cols = pl.ds((g * 8 + 2 * k + h) * 128, 128)
            dq[:, cols] = val[h * 128 : h * 128 + 128].astype(BF16)

    def grad_step(g, k, j):
        if k < 2 and j % 2 == 0:
            grad_keys(g, (4, 0)[k] + j // 4 * 2, j // 2 % 2)
        if k >= 2 and j in (0, 4) and g != 2:
            grad_query(g, 2 * (k - 2) + j // 4)

    def unit(soft=None, ahead=None, grads=None, load=None):
        if ahead is not None:
            g, k = ahead
            cols = [pl.ds((g * 8 + 2 * k + h) * 128, 128) for h in range(2)]
            qb = jnp.concatenate([q[:, i] for i in cols], axis=0)
            gb = jnp.concatenate([gm[:, i] for i in cols], axis=0)
            qx = jnp.concatenate([qb, jnp.concatenate([bias[...]] * 2, axis=0)], axis=1)
            kt, vt = KT[g % 2], VT[g % 2]
            s_ref, dp_ref = S[k % 2], DP[k % 2]
        for j in range(8):
            if load is not None:
                for t in range(2 * j, 2 * j + 2):
                    load_block(load, t)
            if ahead is not None:
                cols = pl.ds(j * 256, 256)
                if j < 4:
                    s_ref[:, cols] = dot(qb, kt[0:128, cols])
                else:
                    s_ref[:, cols] = dot(qx, kt[:, cols])
                dp_ref[:, cols] = dot(gb, vt[:, cols])
            if soft is not None:
                for i in range(2 * j, 2 * j + 2):
                    soft_rows(soft[1] % 2, soft[0] % 2, soft[1], i)
            if grads is not None:
                grad_step(*grads, j)
            if soft is not None and j == 6:
                load_query(*soft)

    def back_copy(g, step):
        return pltpu.make_async_remote_copy(
            src_ref=term.at[g, :, 8 + step], dst_ref=back.at[g, step - 1],
            send_sem=d_send.at[g, step], recv_sem=d_recv.at[g, step],
            device_id=(c - step, r), device_id_type=MESH,
        )

    def send_back(g):
        for step in range(1, 8):
            @pl.when(step <= c)
            def _():
                back_copy(g, step).start()

    def finish_back(g):
        for step in range(1, 8):
            @pl.when(c + step < 8)
            def _():
                wait_bytes(back.at[g, step - 1], d_recv.at[g, step])
        cols = pl.ds(g * 128, 128)
        for kind, ref in ((0, drk_ref), (1, drv_ref)):
            total = term[g, kind, 8].astype(F32)
            for step in range(1, 8):
                total = total + back[g, step - 1, kind].astype(F32)
            ref[:, cols] = total.astype(BF16)

    def half_copy(g):
        return pltpu.make_async_remote_copy(
            src_ref=term.at[g, :, pl.ds(0, 8), other_half], dst_ref=half_in.at[g],
            send_sem=h_send.at[g], recv_sem=h_recv.at[g], device_id=sibling, device_id_type=MESH,
        )

    def z_copy(g, step):
        to_z = (z + step) % 4
        return pltpu.make_async_remote_copy(
            src_ref=half_sum.at[g, :, :, to_z], dst_ref=z_in.at[g, step - 1],
            send_sem=z_send.at[g, step], recv_sem=z_recv.at[g, step],
            device_id=(c, to_z * 4 + y_hi * 2 + core), device_id_type=MESH,
        )

    def add_halves(g):
        wait_bytes(half_in.at[g], h_recv.at[g])
        for kind in range(2):
            total = term[g, kind, pl.ds(0, 8), my_half, :].astype(F32) + half_in[g, kind].astype(F32)
            half_sum[g, kind] = total.astype(BF16).reshape(8, 4, 16, 128)
        for step in range(1, 4):
            z_copy(g, step).start()

    def add_z(g):
        for step in range(1, 4):
            wait_bytes(z_in.at[g, step - 1], z_recv.at[g, step])
        total = half_sum[g, :, :, z].astype(F32)
        for step in range(1, 4):
            total = total + z_in[g, step - 1].astype(F32)
        for cc in range(8):
            for yy in range(2):
                rows = slice(yy * 8, yy * 8 + 8)
                tile = jnp.concatenate([total[0, cc, rows], total[1, cc, rows]], axis=0)
                plane_out[cc, yy, g] = tile.astype(BF16)

    def plane_copy(step, heads, turn):
        to_c, to_y = plane_device(step)
        return pltpu.make_async_remote_copy(
            src_ref=plane_out.at[to_c, to_y, heads], dst_ref=plane_in.at[plane_id, heads],
            send_sem=x_send.at[turn], recv_sem=x_recv.at[turn],
            device_id=(to_c, z * 4 + to_y * 2 + core), device_id_type=MESH,
        )

    def plane_send(first, count, turn):
        heads = pl.ds(first, count)
        for step in range(1, 16):
            plane_copy(step, heads, turn).start()
        plane_in[plane_id, heads] = plane_out[c, y_hi, heads]

    def plane_finish(first, count, turn):
        for sem in (x_recv, x_send):
            wait_bytes(plane_in.at[pl.ds(0, 15), pl.ds(first, count)], sem.at[turn])
        for g in range(first, first + count):
            total = jnp.zeros((16, 128), F32)
            for i in range(16):
                total = total + plane_in[i, g].astype(F32)
            cols = pl.ds(g * 128, 128)
            dpk_ref[:, cols] = total[0:8].astype(BF16)
            dpv_ref[:, cols] = total[8:16].astype(BF16)

    def out_copy(g):
        cols = pl.ds(g * 1024, 1024)
        return pltpu.make_async_copy(dq.at[:, cols], dq_hbm.at[:, cols], out_sem.at[g])

    wait_bytes(prompt_bytes(0), p_recv.at[0])
    send_column(0)
    send_prompt(1)

    row = lax.broadcasted_iota(jnp.int32, (128, 1024), 0)
    key = lax.broadcasted_iota(jnp.int32, (128, 1024), 1)
    flag = ((key == row + 1) & (key < 128)) | ((row == 127) & (key >= (c + 1) * 128))
    flag = jnp.where(flag, 1.0, 0.0).astype(BF16)
    kt0[128:, 1024:] = flag
    kt1[128:, 1024:] = flag
    row = lax.broadcasted_iota(jnp.int32, (128, 128), 0)
    key = lax.broadcasted_iota(jnp.int32, (128, 128), 1)
    bias[...] = jnp.where(key >= row, -1e30, 0.0).astype(BF16)
    for step in range(1, 8):
        @pl.when(step > c)
        def _():
            for g in range(4):
                for kind in range(2):
                    kv[g, kind, 8 + step] = jnp.zeros((128, 128), BF16)

        @pl.when(c + step > 7)
        def _():
            for g in range(4):
                back[g, step - 1] = jnp.zeros((2, 128, 128), BF16)

    q_load.wait()
    g_load.wait()
    live = lax.broadcasted_iota(jnp.int32, (128, 128), 0) + c * 128 < len_ref[0]
    for t in range(32):
        cols = pl.ds(t * 128, 128)
        gm[:, cols] = jnp.where(live, gm[:, cols].astype(F32), 0.0).astype(BF16)

    relays(0, True)
    send_resp(1)
    send_resp(2)
    send_resp(3)
    forward_head(0)
    wait_bytes(prompt_bytes(1), p_recv.at[1])
    send_column(1)
    send_column(2)
    send_column(3)
    relays(1, True)
    await_head(0)
    for t in range(16):
        load_block(0, t)
    unit(ahead=(0, 0))
    for g in range(4):
        for k in range(4):
            if k == 1:
                if g < 3:
                    forward_head(g + 1)
                if g >= 1:
                    send_back(g - 1)
                if g >= 2:
                    add_z(g - 2)
            if (g, k) in RELAY_AT:
                relays(RELAY_AT[g, k], True)
            if k == 2 and g >= 1:
                half_copy(g - 1).start()
            if k == 3:
                if g < 3:
                    await_head(g + 1)
                if g >= 1:
                    add_halves(g - 1)
            last = k == 3
            ahead = (g, k + 1) if not last else (g + 1, 0) if g < 3 else None
            unit(
                soft=(g, k), ahead=ahead, grads=(g - 1, k) if g > 0 else None,
                load=g + 1 if last and g < 3 else None,
            )
        if g in (1, 2):
            out_copy(g - 1).start()

    for i in range(4):
        grad_keys(3, i // 2 * 2, i % 2)
    half_copy(3).start()
    for i in range(4):
        grad_keys(3, 4 + i // 2 * 2, i % 2)
    send_back(3)
    add_halves(3)
    add_z(2)
    plane_send(0, 3, 0)
    for k in range(4):
        grad_query(2, k)
    out_copy(2).start()
    for k in range(4):
        grad_query(3, k)
    out_copy(3).start()
    add_z(3)
    plane_send(3, 1, 1)
    for g in range(3):
        finish_back(g)
    plane_finish(0, 3, 0)
    finish_back(3)
    plane_finish(3, 1, 1)

    for turn in range(2):
        wait_bytes(prompt_bytes(turn), p_send.at[turn])
    for g in range(4):
        wait_bytes(column_bytes(g), a_send.at[g])
        wait_bytes(kv.at[g, :, pl.ds(0, 8), my_half], f_send.at[g])
        wait_bytes(half_in.at[g], h_send.at[g])
        for step in range(1, 4):
            @pl.when(x + step < 4)
            def _():
                wait_bytes(kv.at[g, :, 8], r_send.at[g, step])

        @pl.when(y_lo == 0)
        def _():
            wait_bytes(kv.at[g, :, 8], r_send.at[g, 4])

        relays(g, False)
        for step in range(1, 8):
            @pl.when(step <= c)
            def _():
                wait_bytes(term.at[g, :, 8 + step], d_send.at[g, step])
        for step in range(1, 4):
            wait_bytes(z_in.at[g, step - 1], z_send.at[g, step])
        out_copy(g).wait()


def hand_over(*refs):
    ins, outs, bufs, in_sem, out_sem = refs[:5], refs[5:10], refs[10:15], refs[15], refs[16]
    quarters = [(0, pl.ds(i * 1024, 1024)) for i in range(4)]
    parts = quarters + [(i, pl.ds(0, 512)) for i in range(1, 5)]
    reads = [
        pltpu.make_async_copy(ins[i].at[:, cols], bufs[i].at[:, cols], in_sem.at[n])
        for n, (i, cols) in enumerate(parts)
    ]
    writes = [
        pltpu.make_async_copy(bufs[i].at[:, cols], outs[i].at[:, cols], out_sem.at[n])
        for n, (i, cols) in enumerate(parts)
    ]
    for copy in reads:
        copy.start()
    for read, write in zip(reads, writes):
        read.wait()
        write.start()
    for copy in writes:
        copy.wait()


def per_device(query, prompt_keys, prompt_value_rows, response_keys, response_values, d_out, lengths):
    any_spec = pl.BlockSpec(memory_space=pl.ANY)
    vmem = pl.BlockSpec(memory_space=pltpu.VMEM)
    dma = pltpu.SemaphoreType.DMA
    scratch = [
        pltpu.VMEM((128, 4096), BF16),
        pltpu.VMEM((128, 4096), BF16),
        pltpu.VMEM((128, 4096), BF16),
        pltpu.VMEM((2, 128, 512), BF16),
        pltpu.VMEM((2, 128, 512), F32),
        pltpu.VMEM((4, 2, 16, 128, 128), BF16),
        pltpu.VMEM((4, 2, 16, 128, 128), BF16),
        pltpu.VMEM((4, 7, 2, 128, 128), BF16),
        pltpu.VMEM((4, 2, 8, 64, 128), BF16),
        pltpu.VMEM((4, 2, 8, 4, 16, 128), BF16),
        pltpu.VMEM((4, 3, 2, 8, 16, 128), BF16),
        pltpu.VMEM((8, 2, 4, 16, 128), BF16),
        pltpu.VMEM((16, 4, 16, 128), BF16),
    ]
    scratch += [pltpu.VMEM((1024, 2048), BF16)] * 4
    scratch += [pltpu.VMEM((ROWS, 2048), F32)] * 4
    scratch += [pltpu.VMEM((256, 2048), BF16)] * 2 + [pltpu.VMEM((128, 2048), BF16)] * 2
    scratch += [pltpu.VMEM((128, 1024), BF16)] * 4 + [pltpu.VMEM((128, 128), BF16)]
    scratch += [dma((12,)), dma((4,)), dma((2,)), dma((2,)), dma((4,)), dma((4,)), dma((4,)), dma((4,))]
    scratch += [dma((4, 8))] * 4 + [dma((4,))] * 2 + [dma((4, 4))] * 2 + [dma((2,))] * 2 + [dma((4, 5))]
    out = pl.pallas_call(
        kernel,
        out_shape=[
            jax.ShapeDtypeStruct((128, 4096), BF16),
            jax.ShapeDtypeStruct((128, 512), BF16),
            jax.ShapeDtypeStruct((128, 512), BF16),
            jax.ShapeDtypeStruct((8, 512), BF16),
            jax.ShapeDtypeStruct((8, 512), BF16),
        ],
        in_specs=[any_spec] * 6 + [pl.BlockSpec(memory_space=pltpu.SMEM)],
        out_specs=[any_spec] + [vmem] * 4,
        scratch_shapes=scratch,
        compiler_params=pltpu.CompilerParams(
            collective_id=0, has_side_effects=True, vmem_limit_bytes=62 * 2**20
        ),
    )(query[0], prompt_keys, prompt_value_rows, response_keys[0], response_values[0], d_out[0], lengths)
    d_query, d_rk, d_rv, d_pk, d_pv = pl.pallas_call(
        hand_over,
        out_shape=[jax.ShapeDtypeStruct(a.shape, a.dtype) for a in out],
        in_specs=[any_spec] * 5,
        out_specs=[any_spec] * 5,
        scratch_shapes=[pltpu.VMEM(a.shape, a.dtype) for a in out] + [dma((8,)), dma((8,))],
    )(*out)
    return d_query[None], d_rk[None], d_rv[None], d_pk, d_pv


def solution(mesh):
    return jax.shard_map(
        per_device,
        mesh=mesh,
        in_specs=(
            P("resp", "ctx", None),
            P("ctx", None),
            P("ctx", None),
            P("resp", "ctx", None),
            P("resp", "ctx", None),
            P("resp", "ctx", None),
            P("resp"),
        ),
        out_specs=(
            P("resp", "ctx", None),
            P("resp", "ctx", None),
            P("resp", "ctx", None),
            P(("ctx", "resp"), None),
            P(("ctx", "resp"), None),
        ),
        check_vma=False,
    )
```

time: 77.4 us -> 77.1 us (level)
  Pallas kernels: 75.5 us -> 74.6 us
    pallas_call x1, Pallas kernels: 73.4 us -> 72.4 us  [per_device(): pl.pallas_call(kernel, out_shape=[jax.ShapeDtypeStruct((128, 4096), BF16)...]
where the time goes in v3:
time: 77.1 us; the launch traced here: 76 us
  Pallas kernels  74.6 us (97%)
  between operations  1.47 us (2%)
    pallas_call x1, Pallas kernels, per_device(): pl.pallas_call(kernel, out_shape=[jax.ShapeDtypeStruct((128, 4096), BF16)...  72.4 us
    pallas_call x1, Pallas kernels, per_device(): pl.pallas_call(hand_over, out_shape=[jax.ShapeDtypeStruct(a.shape, a.dtyp...  2.14 us

profile of v3, /device:TPU:0, one launch (start us, length us, event | category | flops | bytes accessed | tf_op | source)
XLA Modules:
  0.0 76.0 jit_solution(3493959928710082667)
XLA Ops:
  1.3 72.4 %shard_map.110 = (bf16[128,4096]{1,0:T(8,128)(2,1)}, bf16[128,512]{1,0:T(8,128)(2,1)}, bf16[128,512]{1,0:T(8,128)(2,1)}, bf16[8,512]{1,0:T(8,128)(2,1)}, bf16[8,512]{1,0:T(8,128)(2,1)}) custom-call(bf16[128,4096]{1,0:T(8,128)(2,1)} %bitcast.7, bf16[128,512]{1,0:T(8,128)(2,1)} %pk_hbm.1, bf16[128,512]{1,0:T(8,128)(2,1)} %pv_hbm.1, bf16[128,512]{1,0:T(8,128)(2,1)} %bitcast.9, ...), custom_call_target="tpu_custom_call" | custom-call | tf_op jit(solution)/shard_map/pallas_call | solution.py:549
  73.7 2.1 %shard_map.111 = (bf16[128,4096]{1,0:T(8,128)(2,1)}, bf16[128,512]{1,0:T(8,128)(2,1)}, bf16[128,512]{1,0:T(8,128)(2,1)}, bf16[8,512]{1,0:T(8,128)(2,1)}, bf16[8,512]{1,0:T(8,128)(2,1)}) custom-call(bf16[128,4096]{1,0:T(8,128)(2,1)} %get-tuple-element.15.refs_0_, bf16[128,512]{1,0:T(8,128)(2,1)} %get-tuple-element.16.refs_1_, ...), custom_call_target="tpu_custom_call" | custom-call | tf_op jit(solution)/shard_map/pallas_call | solution.py:565

commit v4 on v3

--- a/solution.py
+++ b/solution.py
@@ -383,6 +383,7 @@
     send_column(0)
     send_prompt(1)
 
+    relays(0, True)
     row = lax.broadcasted_iota(jnp.int32, (128, 1024), 0)
     key = lax.broadcasted_iota(jnp.int32, (128, 1024), 1)
     flag = ((key == row + 1) & (key < 128)) | ((row == 127) & (key >= (c + 1) * 128))
@@ -411,7 +412,6 @@
         cols = pl.ds(t * 128, 128)
         gm[:, cols] = jnp.where(live, gm[:, cols].astype(F32), 0.0).astype(BF16)
 
-    relays(0, True)
     send_resp(1)
     send_resp(2)
     send_resp(3)

time: 77.1 us -> 77.1 us (level)
  no operation moved by 1% of the time
where the time goes in v4:
time: 77.1 us; the launch traced here: 76 us
  Pallas kernels  74.6 us (97%)
  between operations  1.47 us (2%)
    pallas_call x1, Pallas kernels, per_device(): pl.pallas_call(kernel, out_shape=[jax.ShapeDtypeStruct((128, 4096), BF16)...  72.4 us
    pallas_call x1, Pallas kernels, per_device(): pl.pallas_call(hand_over, out_shape=[jax.ShapeDtypeStruct(a.shape, a.dtyp...  2.14 us

profile of v4, /device:TPU:0, one launch (start us, length us, event | category | flops | bytes accessed | tf_op | source)
XLA Modules:
  0.0 76.0 jit_solution(13919298864387055189)
XLA Ops:
  1.3 72.4 %shard_map.110 = (bf16[128,4096]{1,0:T(8,128)(2,1)}, bf16[128,512]{1,0:T(8,128)(2,1)}, bf16[128,512]{1,0:T(8,128)(2,1)}, bf16[8,512]{1,0:T(8,128)(2,1)}, bf16[8,512]{1,0:T(8,128)(2,1)}) custom-call(bf16[128,4096]{1,0:T(8,128)(2,1)} %bitcast.7, bf16[128,512]{1,0:T(8,128)(2,1)} %pk_hbm.1, bf16[128,512]{1,0:T(8,128)(2,1)} %pv_hbm.1, bf16[128,512]{1,0:T(8,128)(2,1)} %bitcast.9, ...), custom_call_target="tpu_custom_call" | custom-call | tf_op jit(solution)/shard_map/pallas_call | solution.py:549
  73.7 2.1 %shard_map.111 = (bf16[128,4096]{1,0:T(8,128)(2,1)}, bf16[128,512]{1,0:T(8,128)(2,1)}, bf16[128,512]{1,0:T(8,128)(2,1)}, bf16[8,512]{1,0:T(8,128)(2,1)}, bf16[8,512]{1,0:T(8,128)(2,1)}) custom-call(bf16[128,4096]{1,0:T(8,128)(2,1)} %get-tuple-element.15.refs_0_, bf16[128,512]{1,0:T(8,128)(2,1)} %get-tuple-element.16.refs_1_, ...), custom_call_target="tpu_custom_call" | custom-call | tf_op jit(solution)/shard_map/pallas_call | solution.py:565
